TPU v7x, 512 devices: a whole 4x4x16 slice. The times are simulated.
512 devices in a mesh: feat: 64 (over z_lo, y, core), tok: 8 (over z_hi, x).
Axes of the slice: x: 4, y: 4, z: 16 (z_hi: 2, z_lo: 8; z = z_hi * 8 + z_lo), core: 2. Of those that a mesh axis runs over, the one named last changes fastest.
Arguments:
- source: bfloat16 [1024, 3584], P(('tok', 'feat')), may hold values from -6 to 6
- target: bfloat16 [1024, 3584], P(('tok', 'feat')), may hold values from -6 to 6
- enc_weight: bfloat16 [3584, 16384], P('tok', 'feat'), may hold values from -0.09375 to 0.09375
- enc_bias: float32 [16384], P('feat'), may hold values from -3 to 3
- dec_weight: bfloat16 [16384, 3584], P('feat', 'tok'), may hold values from -0.09375 to 0.09375
- active: int32 [1024, 16384], P('tok', 'feat'), may hold values 0 or 1
Outputs:
- recon_error: float32 [1024, 3584], P(('tok', 'feat'))
- grad_enc: bfloat16 [3584, 16384], P(None, 'feat')
- grad_bias: float32 [16384], P('feat')
- grad_dec: bfloat16 [16384, 3584], P('feat')
All inputs are finite; a program needn't handle non-finite values. No bound on the sum of `active` on one device may be relied on, other than what follows from the above.
Results may differ from a plain program's by a relative error of at most 0.019.
Values may be sent and summed in bfloat16 or wider, within the bound.
A program may use at most 64 MiB of HBM per device.

v0:
```python
import math
import jax
import jax.numpy as jnp
from jax import lax
from jax.sharding import PartitionSpec as P


def on_device(source, target, enc_weight, enc_bias, dec_weight, active):
    row_count = source.shape[0]
    group_rows = row_count * lax.axis_size("feat")
    token_total = group_rows * lax.axis_size("tok")
    gathered = lax.all_gather(source, "feat", axis=0, tiled=True)
    slab_rows = gathered
    preact = (
        jnp.dot(
            slab_rows,
            lax.all_gather(enc_weight, "tok", axis=0, tiled=True),
            preferred_element_type=jnp.float32,
        )
        + enc_bias
    )
    gating = active.astype(jnp.float32)
    features = (gating * preact).astype(jnp.bfloat16)
    full_dec = lax.all_gather(dec_weight, "tok", axis=1, tiled=True)
    slab_rows = features
    recon = lax.psum_scatter(
        jnp.dot(slab_rows, full_dec, preferred_element_type=jnp.float32),
        "feat",
        scatter_dimension=0,
        tiled=True,
    )
    recon_error = recon - target.astype(jnp.float32)
    signal = (recon_error * (1.0 / math.sqrt(token_total))).astype(jnp.bfloat16)
    signal_all = lax.all_gather(signal, "feat", axis=0, tiled=True)
    dec_part = lax.dot_general(
        features, signal_all, (((0,), (0,)), ((), ())), preferred_element_type=jnp.float32
    )
    backflow = lax.dot_general(
        signal_all, full_dec, (((1,), (1,)), ((), ())), preferred_element_type=jnp.float32
    )
    pre_grad = gating * backflow
    pre_round = pre_grad.astype(jnp.bfloat16)
    bias_part = jnp.sum(pre_grad, axis=0).astype(jnp.bfloat16)
    enc_part = lax.dot_general(
        gathered, pre_round, (((0,), (0,)), ((), ())), preferred_element_type=jnp.float32
    )
    enc_half = enc_part.astype(jnp.bfloat16)
    dec_half = dec_part.astype(jnp.bfloat16)
    enc_summed, dec_summed, bias_summed = (
        lax.psum(enc_half, "tok").astype(jnp.float32),
        lax.psum(dec_half, "tok").astype(jnp.float32),
        lax.psum(bias_part, "tok").astype(jnp.float32),
    )
    enc_out = enc_summed.astype(jnp.bfloat16)
    dec_out = dec_summed.astype(jnp.bfloat16)
    return (recon_error, enc_out, bias_summed, dec_out)


def solution(mesh):
    placed = (
        P(("tok", "feat"), None),
        P(("tok", "feat"), None),
        P("tok", "feat"),
        P("feat"),
        P("feat", "tok"),
        P("tok", "feat"),
    )
    return jax.shard_map(
        on_device,
        mesh=mesh,
        in_specs=placed,
        out_specs=(P(("tok", "feat"), None), P(None, "feat"), P("feat"), P("feat", None)),
        check_vma=False,
    )
```

profile of v0, /device:TPU:14, one launch (start us, length us, event | category | flops | bytes accessed | tf_op | source)
XLA Modules:
  0.0 1527.0 jit_solution(12357005956135973958)
XLA Ops:
  7.2 0.0 copy-start.2
  7.2 0.0 copy-start.4
  7.2 0.0 all-gather.5.cloned.1.call-start
  7.2 0.7 all-gather.5.cloned.1.call-update
  7.9 0.0 all-gather.7.cloned.1.call-start
  8.0 0.7 all-gather.7.cloned.1.call-update
  8.7 0.0 all-reduce.5.cloned.1.call-start
  8.7 148.6 %all-gather = bf16[64,2,3584]{2,1,0:T(2,128)(2,1)S(1)} all-gather(bf16[1,2,3584]{2,1,0:T(2,128)(2,1)} %bitcast.16), channel_id=1, replica_groups=mesh['feat'=64,'tok'=8] {'feat'}, dimensions={0}, use_global_device_ids=true | all-gather | bytes 931840 | tf_op jit(solution)/shard_map/all_gather | solution.py:12
  157.3 0.3 reshape.10
  157.7 0.0 all-gather.5.cloned.1.call-done
  157.7 0.0 copy-done.2
  157.7 0.0 copy-done.4
  157.7 1.9 fusion.2
  159.7 75.7 %all-gather.7.cloned.1.call-done = bf16[256,3584]{0,1:T(8,128)(2,1)} async-done(((bf16[256,448]{0,1:T(8,128)(2,1)}), bf16[256,3584]{0,1:T(8,128)(2,1)}) %all-gather.7.cloned.1.call-update) | async-done | bytes 1835024 | tf_op jit(solution)/shard_map/all_gather | solution.py:24
  235.3 3.5 fusion.6
  238.8 0.0 copy-start.3
  238.8 0.0 all-reduce.5.cloned.1.call-update
  238.8 0.0 all-reduce.7.cloned.1.call-start
  238.9 1.3 dynamic-slice
  240.8 810.8 %all-reduce.5.cloned.1.call-done = f32[128,3584]{1,0:T(8,128)} async-done(((f32[128,3584]{1,0:T(8,128)}), f32[128,3584]{1,0:T(8,128)}) %all-reduce.5.cloned.1.call-update) | async-done | bytes 1835024
  1051.6 0.0 copy-done.3
  1051.6 1.5 fusion.4
  1053.1 116.8 %all-gather.1 = bf16[64,2,3584]{2,1,0:T(2,128)(2,1)S(1)} all-gather(bf16[1,2,3584]{2,1,0:T(2,128)(2,1)S(1)} %get-tuple-element.14), channel_id=1, replica_groups=mesh['feat'=64,'tok'=8] {'feat'}, dimensions={0}, use_global_device_ids=true | all-gather | bytes 931840 | tf_op jit(solution)/shard_map/all_gather | solution.py:34
  1169.9 0.3 reshape.12
  1170.3 0.0 copy-start
  1170.3 1.9 convolution_convert_fusion
  1172.2 0.0 copy-done
  1172.2 0.4 fusion.5
  1172.6 1.9 fusion
  1174.5 0.0 all-reduce.7.cloned.1.call-update
  1174.5 39.5 %psum.22 = bf16[256]{0:T(256)(128)(2,1)S(1)} all-reduce(bf16[256]{0:T(256)(128)(2,1)S(1)} %get-tuple-element.16), channel_id=1, replica_groups=mesh['feat'=64,'tok'=8] {'tok'}, use_global_device_ids=true, to_apply=%region_3.0 | all-reduce | flops 256 | bytes 1024 | tf_op jit(solution)/shard_map/psum | solution.py:52
  1214.1 0.6 convert_element_type.42
  1214.6 300.7 %all-reduce.7.cloned.1.call-done = (bf16[3584,256]{0,1:T(8,128)(2,1)}, bf16[256,3584]{1,0:T(8,128)(2,1)}) async-done(((bf16[3584,256]{0,1:T(8,128)(2,1)}, bf16[256,3584]{1,0:T(8,128)(2,1)}), (bf16[3584,256]{0,1:T(8,128)(2,1)}, bf16[256,3584]{1,0:T(8,128)(2,1)})) %all-reduce.7.cloned.1.call-update) | async-done | bytes 3670032 | tf_op jit(solution)/shard_map/psum | solution.py:50
  1515.3 0.0 copy-start.1
  1515.3 3.9 copy.11
  1519.2 0.0 copy-done.1
  1519.3 1.2 copy.15
Async XLA Ops:
  7.2 150.6 %copy-start.2 = (s32[128,256]{1,0:T(8,128)S(1)}, s32[128,256]{1,0:T(8,128)}, u32[]{:S(2)}) copy-start(s32[128,256]{1,0:T(8,128)} %param.11) | copy-start | bytes 393220
  7.2 150.6 %copy-start.4 = (f32[256]{0:T(256)S(1)}, f32[256]{0:T(256)}, u32[]{:S(2)}) copy-start(f32[256]{0:T(256)} %param.9) | copy-start | bytes 3076
  7.2 150.5 %all-gather.5.cloned.1.call-start = ((), (), s32[]{:S(2)}) async-start(), calls=%async_computation | async-start | bytes 2064384 | tf_op jit(solution)/shard_map/all_gather | solution.py:17
  7.9 227.4 %all-gather.7.cloned.1.call-start = ((), (), s32[]{:S(2)}) async-start(), calls=%async_computation.1 | async-start | bytes 2064384 | tf_op jit(solution)/shard_map/all_gather | solution.py:24
  8.7 1042.9 %all-reduce.5.cloned.1.call-start = ((), (), s32[]{:S(2)}) async-start(), calls=%async_computation.2 | async-start | bytes 3670016
  238.8 812.8 %copy-start.3 = (bf16[2,3584]{1,0:T(2,128)(2,1)S(1)}, bf16[2,3584]{1,0:T(2,128)(2,1)}, u32[]{:S(2)}) copy-start(bf16[2,3584]{1,0:T(2,128)(2,1)} %param.7) | copy-start | bytes 43012
  238.8 1276.5 %all-reduce.7.cloned.1.call-start = ((), (), s32[]{:S(2)}) async-start(), calls=%async_computation.3 | async-start | bytes 7340032 | tf_op jit(solution)/shard_map/psum | solution.py:50
  1170.3 1.9 copy-start
  1515.3 3.9 copy-start.1
Sparse Core Ops, SparseCore 0:
  11.2 116.1 all-gather.4
  130.5 104.7 all-gather.6
  238.9 812.6 all-reduce.4
  1174.7 340.6 all-reduce.6
where the time goes:
time: 1530 us
  waiting for transfers between devices  1190 us (78%)
  blocking collectives  305 us (20%)
    unnamed x5, waiting for transfers between devices  812 us
    psum x1, waiting for transfers between devices, on_device(): lax.psum(enc_half, 'tok').astype(jnp.float32)  301 us
    all_gather x1, blocking collectives, on_device(): gathered = lax.all_gather(source, 'feat', axis=0, tiled=True)  149 us
    all_gather x1, blocking collectives, on_device(): signal_all = lax.all_gather(signal, 'feat', axis=0, tiled=True)  117 us
    all_gather x1, waiting for transfers between devices, on_device(): full_dec = lax.all_gather(dec_weight, 'tok', axis=1, tiled=True)  75.7 us
    psum x1, blocking collectives, on_device(): lax.psum(bias_part, 'tok').astype(jnp.float32)  39.5 us
  transfers between devices with their start and end apart: 4, of which 3 were waited for; matrix products, arithmetic and copies ran while one was open for 0% of the time, Pallas kernels for 0%

commit v1 on v0

--- a/solution.py
+++ b/solution.py
@@ -47,7 +47,7 @@
     enc_half = enc_part.astype(jnp.bfloat16)
     dec_half = dec_part.astype(jnp.bfloat16)
     enc_summed, dec_summed, bias_summed = (
-        lax.psum(enc_half, "tok").astype(jnp.float32),
+        jnp.sum(lax.all_gather(enc_half, "tok"), axis=0).astype(jnp.float32),
         lax.psum(dec_half, "tok").astype(jnp.float32),
         lax.psum(bias_part, "tok").astype(jnp.float32),
     )

time: 1530 us -> 1880 us (1.23)
  the two profiles are of different devices: /device:TPU:14 before, /device:TPU:6 now
where the time goes in v1:
time: 1880 us
  waiting for transfers between devices  1520 us (81%)
  blocking collectives  304 us (16%)
    unnamed x6, waiting for transfers between devices  816 us
    all_gather x1, waiting for transfers between devices, on_device(): lax.all_gather(enc_half, 'tok')  420 us
    psum x1, waiting for transfers between devices, on_device(): lax.psum(dec_half, 'tok').astype(jnp.float32)  212 us
    all_gather x1, blocking collectives, on_device(): gathered = lax.all_gather(source, 'feat', axis=0, tiled=True)  148 us
    all_gather x1, blocking collectives, on_device(): signal_all = lax.all_gather(signal, 'feat', axis=0, tiled=True)  120 us
    all_gather x1, waiting for transfers between devices, on_device(): full_dec = lax.all_gather(dec_weight, 'tok', axis=1, tiled=True)  74.9 us
  transfers between devices with their start and end apart: 5, of which 4 were waited for; matrix products, arithmetic and copies ran while one was open for 2% of the time, Pallas kernels for 0%

profile of v1, /device:TPU:6, one launch (start us, length us, event | category | flops | bytes accessed | tf_op | source)
XLA Modules:
  0.0 1883.4 jit_solution(17829285295520499153)
XLA Ops:
  7.2 0.0 copy-start
  7.2 0.0 copy-start.2
  7.2 0.0 all-gather.7.cloned.1.call-start
  7.2 0.7 all-gather.7.cloned.1.call-update
  7.9 0.0 all-gather.9.cloned.1.call-start
  8.0 0.7 all-gather.9.cloned.1.call-update
  8.7 0.0 all-reduce.6.cloned.1.call-start
  8.7 147.5 %all-gather.1 = bf16[64,2,3584]{2,1,0:T(2,128)(2,1)S(1)} all-gather(bf16[1,2,3584]{2,1,0:T(2,128)(2,1)} %bitcast.22), channel_id=1, replica_groups=mesh['feat'=64,'tok'=8] {'feat'}, dimensions={0}, use_global_device_ids=true | all-gather | bytes 931840 | tf_op jit(solution)/shard_map/all_gather | solution.py:12
  156.2 0.3 reshape.11
  156.6 0.0 all-gather.7.cloned.1.call-done
  156.6 0.0 copy-done
  156.6 0.0 copy-done.2
  156.6 1.9 fusion.2
  158.6 74.9 %all-gather.9.cloned.1.call-done = bf16[256,3584]{0,1:T(8,128)(2,1)} async-done(((bf16[256,448]{0,1:T(8,128)(2,1)}), bf16[256,3584]{0,1:T(8,128)(2,1)}) %all-gather.9.cloned.1.call-update) | async-done | bytes 1835024 | tf_op jit(solution)/shard_map/all_gather | solution.py:24
  233.5 3.5 fusion.6
  236.9 0.0 copy-start.1
  236.9 0.0 all-reduce.6.cloned.1.call-update
  236.9 0.0 all-gather.11.cloned.1.call-start
  237.0 1.3 dynamic-slice
  238.9 814.5 %all-reduce.6.cloned.1.call-done = f32[128,3584]{1,0:T(8,128)} async-done(((f32[128,3584]{1,0:T(8,128)}), f32[128,3584]{1,0:T(8,128)}) %all-reduce.6.cloned.1.call-update) | async-done | bytes 1835024
  1053.5 0.0 copy-done.1
  1053.5 1.5 fusion.4
  1055.0 120.4 %all-gather.2 = bf16[64,2,3584]{2,1,0:T(2,128)(2,1)S(1)} all-gather(bf16[1,2,3584]{2,1,0:T(2,128)(2,1)S(1)} %get-tuple-element.8), channel_id=1, replica_groups=mesh['feat'=64,'tok'=8] {'feat'}, dimensions={0}, use_global_device_ids=true | all-gather | bytes 931840 | tf_op jit(solution)/shard_map/all_gather | solution.py:34
  1175.4 0.3 reshape.13
  1175.8 1.9 fusion.5
  1177.7 1.9 fusion
  1179.6 0.0 all-gather.11.cloned.1.call-update
  1179.6 0.0 all-reduce.4.cloned.1.call-start
  1179.7 1.9 convolution_convert_fusion
  1181.6 0.0 all-reduce.4.cloned.1.call-update
  1181.6 36.2 %psum.14 = bf16[256]{0:T(256)(128)(2,1)S(1)} all-reduce(bf16[256]{0:T(256)(128)(2,1)S(1)} %get-tuple-element.10), channel_id=1, replica_groups=mesh['feat'=64,'tok'=8] {'tok'}, use_global_device_ids=true, to_apply=%region_3.0 | all-reduce | flops 256 | bytes 1024 | tf_op jit(solution)/shard_map/psum | solution.py:52
  1217.8 0.6 convert_element_type.44
  1218.4 420.0 %all-gather.11.cloned.1.call-done = bf16[28672,256]{0,1:T(8,128)(2,1)} async-done(((bf16[3584,256]{0,1:T(8,128)(2,1)}), bf16[28672,256]{0,1:T(8,128)(2,1)}) %all-gather.11.cloned.1.call-update) | async-done | bytes 14680080 | tf_op jit(solution)/shard_map/all_gather | solution.py:50
  1638.4 10.8 copy.11
  1649.2 11.0 bitcast_reduce_fusion
  1660.2 2.3 copy.10
  1662.5 211.5 %all-reduce.4.cloned.1.call-done = bf16[256,3584]{1,0:T(8,128)(2,1)} async-done(((bf16[256,3584]{1,0:T(8,128)(2,1)}), bf16[256,3584]{1,0:T(8,128)(2,1)}) %all-reduce.4.cloned.1.call-update) | async-done | bytes 1835024 | tf_op jit(solution)/shard_map/psum | solution.py:51
  1874.0 2.8 copy.14
Async XLA Ops:
  7.2 149.5 %copy-start = (s32[128,256]{1,0:T(8,128)S(1)}, s32[128,256]{1,0:T(8,128)}, u32[]{:S(2)}) copy-start(s32[128,256]{1,0:T(8,128)} %param.11) | copy-start | bytes 393220
  7.2 149.5 %copy-start.2 = (f32[256]{0:T(256)S(1)}, f32[256]{0:T(256)}, u32[]{:S(2)}) copy-start(f32[256]{0:T(256)} %param.9) | copy-start | bytes 3076
  7.2 149.4 %all-gather.7.cloned.1.call-start = ((), (), s32[]{:S(2)}) async-start(), calls=%async_computation | async-start | bytes 2064384 | tf_op jit(solution)/shard_map/all_gather | solution.py:17
  7.9 225.5 %all-gather.9.cloned.1.call-start = ((), (), s32[]{:S(2)}) async-start(), calls=%async_computation.1 | async-start | bytes 2064384 | tf_op jit(solution)/shard_map/all_gather | solution.py:24
  8.7 1044.8 %all-reduce.6.cloned.1.call-start = ((), (), s32[]{:S(2)}) async-start(), calls=%async_computation.4 | async-start | bytes 3670016
  236.9 816.5 %copy-start.1 = (bf16[2,3584]{1,0:T(2,128)(2,1)S(1)}, bf16[2,3584]{1,0:T(2,128)(2,1)}, u32[]{:S(2)}) copy-start(bf16[2,3584]{1,0:T(2,128)(2,1)} %param.7) | copy-start | bytes 43012
  236.9 1401.5 %all-gather.11.cloned.1.call-start = ((), (), s32[]{:S(2)}) async-start(), calls=%async_computation.3 | async-start | bytes 16515072 | tf_op jit(solution)/shard_map/all_gather | solution.py:50
  1179.6 694.4 %all-reduce.4.cloned.1.call-start = ((), (), s32[]{:S(2)}) async-start(), calls=%async_computation.2 | async-start | bytes 3670016 | tf_op jit(solution)/shard_map/psum | solution.py:51
Sparse Core Ops, SparseCore 0:
  11.2 117.5 all-gather.6
  132.0 101.3 all-gather.8
  237.1 816.3 all-reduce.5
  1179.7 458.6 all-gather.10
  1641.5 232.4 all-reduce.3
